TPU v7x, 32 devices: a whole 2x2x4 slice. The times are simulated.
32 devices in a mesh: grp: 4 (over x, core), tp: 8 (over z, y).
Axes of the slice: x: 2, y: 2, z: 4, core: 2. Of those that a mesh axis runs over, the one named last changes fastest.
Arguments:
- teacher_hidden: bfloat16 [384, 8192], P(('grp', 'tp')), may hold values from -150 to 150
- teacher_head: bfloat16 [8192, 98304], P(None, ('grp', 'tp')), may hold values from -0.0625 to 0.0625
- student_hidden: bfloat16 [384, 3584], P(('grp', 'tp')), may hold values from -150 to 150
- student_head: bfloat16 [3584, 98304], P(None, ('grp', 'tp')), may hold values from -0.09375 to 0.09375
- labels: int32 [384], replicated, may hold values from 0 to 98303
- owner_map: int32 [384], replicated, may hold values from 0 to 383, each once
Outputs:
- token_loss: float32 [384], P(('grp', 'tp'))
- grad_head: bfloat16 [3584, 98304], P(None, ('grp', 'tp'))
- grad_hidden: bfloat16 [384, 3584], P(('grp', 'tp'))
Inputs may be any that keep to these rules, and one draw needn't show every extreme that they name: owner_map holds each of 0 to 383 once.
All inputs are finite; a program needn't handle non-finite values.
Results may differ from a plain program's by a relative error of at most 0.0085.
Values may be sent and summed in bfloat16 or wider, within the bound.
A program may use at most 192 MiB of HBM per device.

v0:
```python
import math

import jax
import jax.numpy as jnp
from jax import lax
from jax.sharding import PartitionSpec as P

VOCABULARY = 98304
TOKENS = 384


def row_terms(teacher_rows, student_rows, teacher_lse, student_lse, weight, reverse, hits):
    log_teacher = teacher_rows - teacher_lse[:, None]
    log_student = student_rows - student_lse[:, None]
    teacher_prob = jnp.exp(log_teacher)
    student_prob = jnp.exp(log_student)
    mixed = weight[:, None] * (student_prob - teacher_prob)
    mixed = mixed + (1.0 - weight)[:, None] * student_prob * (
        log_student - log_teacher - reverse[:, None]
    )
    mixed = mixed + student_prob - hits.astype(jnp.float32)
    return (mixed / TOKENS).astype(jnp.bfloat16)


def shards(teacher_hidden, teacher_head, student_hidden, student_head, labels, owner_map):
    rows = student_hidden.shape[0]
    vocab_local = teacher_head.shape[1]
    position = lax.axis_index(("grp", "tp"))
    teacher_logits = jnp.dot(
        lax.all_gather(teacher_hidden, ("grp", "tp"), axis=0, tiled=True),
        teacher_head,
        preferred_element_type=jnp.float32,
    )
    student_full = lax.all_gather(student_hidden, ("grp", "tp"), axis=0, tiled=True)
    teacher_logits = jnp.take(teacher_logits, owner_map, axis=0)
    student_logits = jnp.dot(student_full, student_head, preferred_element_type=jnp.float32)
    vocab_ids = position * vocab_local + lax.iota(jnp.int32, vocab_local)
    hits = labels[:, None] == vocab_ids[None, :]
    teacher_top, student_top = lax.pmax(
        (jnp.max(teacher_logits, axis=1), jnp.max(student_logits, axis=1)), ("grp", "tp")
    )
    teacher_exp = jnp.exp(teacher_logits - teacher_top[:, None])
    student_exp = jnp.exp(student_logits - student_top[:, None])
    differ = teacher_logits - student_logits
    teacher_total, student_total, teacher_moment, forward_moment, reverse_moment, label_logit = (
        lax.psum(
            (
                jnp.sum(teacher_exp, axis=1),
                jnp.sum(student_exp, axis=1),
                jnp.sum(teacher_exp * teacher_logits, axis=1),
                jnp.sum(teacher_exp * differ, axis=1),
                jnp.sum(student_exp * differ, axis=1),
                jnp.sum(jnp.where(hits, student_logits, 0.0), axis=1),
            ),
            ("grp", "tp"),
        )
    )
    teacher_lse = teacher_top + jnp.log(teacher_total)
    student_lse = student_top + jnp.log(student_total)
    entropy = teacher_lse - teacher_moment / teacher_total
    weight = entropy / math.log(VOCABULARY)
    forward = forward_moment / teacher_total - teacher_lse + student_lse
    reverse = -reverse_moment / student_total - student_lse + teacher_lse
    cross = student_lse - label_logit
    loss_all = weight * forward + (1.0 - weight) * reverse + cross
    grad_logits = row_terms(
        teacher_logits, student_logits, teacher_lse, student_lse, weight, reverse, hits
    )
    token_loss = lax.dynamic_slice_in_dim(loss_all, position * rows, rows)
    grad_head = lax.dot_general(
        student_full, grad_logits, (((0,), (0,)), ((), ())), preferred_element_type=jnp.float32
    ).astype(jnp.bfloat16)
    grad_hidden = lax.psum_scatter(
        lax.dot_general(
            grad_logits, student_head, (((1,), (1,)), ((), ())), preferred_element_type=jnp.float32
        ),
        ("grp", "tp"),
        scatter_dimension=0,
        tiled=True,
    )
    return (token_loss, grad_head, grad_hidden.astype(jnp.bfloat16))


def solution(mesh):
    in_specs = (
        P(("grp", "tp"), None),
        P(None, ("grp", "tp")),
        P(("grp", "tp"), None),
        P(None, ("grp", "tp")),
        P(),
        P(),
    )
    out_specs = (P(("grp", "tp")), P(None, ("grp", "tp")), P(("grp", "tp"), None))
    return jax.shard_map(shards, mesh=mesh, in_specs=in_specs, out_specs=out_specs, check_vma=False)
```

profile of v0, /device:TPU:0, one launch (start us, length us, event | category | flops | bytes accessed | tf_op | source)
XLA Modules:
  0.0 568.4 jit_solution(13252688938735036341)
XLA Ops:
  7.2 0.0 all-gather.7.cloned.1.call-start
  7.2 0.7 all-gather.7.cloned.1.call-update
  7.9 0.0 all-gather.5.cloned.1.call-start
  7.9 0.7 all-gather.5.cloned.1.call-update
  8.7 0.7 compare_select_fusion.1
  9.4 0.0 copy-start
  9.4 0.7 compare_and_fusion
  10.1 0.0 copy-start.3
  10.1 64.1 %all-gather.7.cloned.1.call-done = bf16[32,12,3584]{2,1,0:T(8,128)(2,1)} async-done(((bf16[1,12,3584]{2,1,0:T(8,128)(2,1)}), bf16[32,12,3584]{2,1,0:T(8,128)(2,1)}) %all-gather.7.cloned.1.call-update) | async-done | bytes 2752528 | tf_op jit(solution)/shard_map/all_gather | solution.py:34
  74.1 3.8 reshape.35
  77.9 14.5 %fusion.13 = (f32[384]{0:T(512)S(1)}, f32[384,3072]{1,0:T(8,128)}) fusion(bf16[384,3584]{1,0:T(8,128)(2,1)S(1)} %reshape.35, bf16[3584,3072]{1,0:T(8,128)(2,1)} %param.9), kind=kOutput, calls=%fused_computation.33 | convolution fusion | flops 8456896000 | bytes 29492736 | tf_op jit(solution)/shard_map/dot_general | solution.py:36
  92.4 60.8 %all-gather.5.cloned.1.call-done = bf16[32,12,8192]{2,1,0:T(8,128)(2,1)} async-done(((bf16[1,12,8192]{2,1,0:T(8,128)(2,1)}), bf16[32,12,8192]{2,1,0:T(8,128)(2,1)}) %all-gather.5.cloned.1.call-update) | async-done | bytes 6291472 | tf_op jit(solution)/shard_map/all_gather | solution.py:30
  153.3 8.7 %reshape.33 = bf16[384,8192]{1,0:T(8,128)(2,1)} reshape(bf16[32,12,8192]{2,1,0:T(8,128)(2,1)} %all-gather.5.cloned.1.call-done) | data formatting | bytes 12582912
  162.0 28.6 %fusion.14 = f32[384,3072]{1,0:T(8,128)} fusion(bf16[384,8192]{1,0:T(8,128)(2,1)} %reshape.33, bf16[8192,3072]{1,0:T(8,128)(2,1)} %param.7), kind=kOutput, calls=%fused_computation.34 | convolution fusion | flops 19327352832 | bytes 61341696 | tf_op jit(solution)/shard_map/dot_general | solution.py:29
  190.6 9.1 %gather_fusion = f32[384,3072]{1,0:T(8,128)} fusion(f32[384,3072]{1,0:T(8,128)} %fusion.14, s32[1024]{0:T(1024)S(1)} %pad_clamp_fusion), kind=kCustom, calls=%fused_computation | custom fusion | bytes 9438720 | tf_op jit(solution)/shard_map/jit(_take)/gather | solution.py:35
  199.7 0.0 copy-start.7
  199.7 2.8 select_reduce_fusion
  202.6 39.4 %all-reduce.3 = (f32[384]{0:T(512)S(1)}, f32[384]{0:T(512)S(1)}) all-reduce(f32[384]{0:T(512)S(1)} %get-tuple-element.39, f32[384]{0:T(512)S(1)} %select_reduce_fusion), channel_id=1, replica_groups=mesh['grp'=4,'tp'=8] {'grp','tp'}, use_global_device_ids=true, to_apply=%region_9.10 | all-reduce | flops 768 | bytes 6144 | tf_op jit(solution)/shard_map/pmax | solution.py:39
  242.0 0.0 copy-done.7
  242.0 6.0 %multiply_reduce_fusion.1 = (f32[384]{0:T(512)S(1)}, f32[384]{0:T(512)S(1)}, f32[384]{0:T(512)S(1)}, f32[384]{0:T(512)S(1)}, f32[384]{0:T(512)S(1)}, /*index=5*/f32[384]{0:T(512)S(1)}) fusion(f32[384,3072]{1,0:T(8,128)} %gather_fusion, f32[384,3072]{1,0:T(8,128)} %get-tuple-element.40, f32[384]{0:T(512)S(1)} %get-tuple-element.25, ...), kind=kLoop, calls=%fused_computation.13 | loop fusion | flops 17692416 | bytes 9463680 | tf_op jit(solution)/shard_map/reduce_sum | solution.py:51
  248.0 40.2 %all-reduce.2 = (f32[384]{0:T(512)S(1)}, f32[384]{0:T(512)S(1)}, f32[384]{0:T(512)S(1)}, f32[384]{0:T(512)S(1)}, f32[384]{0:T(512)S(1)}, /*index=5*/f32[384]{0:T(512)S(1)}) all-reduce(f32[384]{0:T(512)S(1)} %get-tuple-element.16, f32[384]{0:T(512)S(1)} %get-tuple-element.17, ...), channel_id=1, replica_groups=mesh['grp'=4,'tp'=8] {'grp','tp'}, use_global_device_ids=true, to_apply=%region_11.12 | all-reduce | flops 2304 | bytes 18432 | tf_op jit(solution)/shard_map/psum | solution.py:46
  288.2 0.0 copy-start.1
  288.2 0.0 copy-start.2
  288.2 0.0 copy-start.4
  288.2 0.6 subtract_add_fusion
  288.8 0.0 copy-start.5
  288.8 0.0 copy-start.6
  288.8 0.0 copy-done
  288.8 0.0 copy-done.3
  288.8 0.0 copy-done.1
  288.9 0.0 copy-done.2
  288.9 0.0 copy-done.4
  288.9 0.5 copy-done.5
  289.4 0.0 copy-done.6
  289.4 22.2 %fusion.9 = f32[384,3584]{1,0:T(8,128)} fusion(bf16[3584,3072]{1,0:T(8,128)(2,1)} %param.9, f32[384,3072]{1,0:T(8,128)} %get-tuple-element.40, f32[384,3072]{1,0:T(8,128)} %gather_fusion, f32[384]{0:T(512)S(1)} %get-tuple-element.30, f32[384]{0:T(512)S(1)} %get-tuple-element.26, f32[384]{0:T(512)S(1)} %get-tuple-element.28, f32[384]{0:T(512)S(1)} %get-tuple-element.31, ...), kind=kOutput, calls=%fused_computation.31 | convolution fusion | flops 8474591232 | bytes 36984192 | tf_op jit(solution)/shard_map/dot_general | solution.py:74
  311.6 160.4 %fusion = f32[16,3584]{1,0:T(8,128)S(1)} fusion(f32[384,3584]{1,0:T(8,128)} %fusion.9), kind=kCustom, calls=%all-reduce-scatter | all-reduce-scatter fusion | flops 1835009 | bytes 5734400
  472.1 1.8 collective-permute-start.1
  473.9 4.9 collective-permute-start.2
  478.9 1.3 collective-permute-start.7
  480.2 4.9 collective-permute-start.3
  485.1 4.8 collective-permute-start.4
  489.9 0.0 collective-permute-done.7
  489.9 2.2 collective-permute-start.5
  492.0 0.0 collective-permute-done.1
  492.0 3.6 collective-permute-start.6
  495.6 0.0 collective-permute-done.2
  495.6 2.5 collective-permute-start
  498.1 24.6 %fusion.1 = bf16[3584,3072]{0,1:T(8,128)(2,1)} fusion(bf16[384,3584]{1,0:T(8,128)(2,1)S(1)} %reshape.35, f32[384,3072]{1,0:T(8,128)} %get-tuple-element.40, f32[384,3072]{1,0:T(8,128)} %gather_fusion, f32[384]{0:T(512)} %copy-done.5, f32[384]{0:T(512)} %copy-done.4, f32[384]{0:T(512)} %copy-done.2, f32[384]{0:T(512)} %copy-done.6, f32[384]{0:T(512)} %copy-done.1, ...), kind=kOutput, calls=%fused_computation.2 | convolution fusion | flops 8485601280 | bytes 34231680 | tf_op jit(solution)/shard_map/dot_general | solution.py:70
  522.7 28.6 %copy.11 = bf16[3584,3072]{1,0:T(8,128)(2,1)} copy(bf16[3584,3072]{0,1:T(8,128)(2,1)} %fusion.1) | data formatting | bytes 44040192
  551.3 1.3 dynamic_slice.3
  552.6 0.0 collective-permute-done.3
  552.6 0.0 collective-permute-done.4
  552.6 0.0 collective-permute-done.5
  552.6 0.0 collective-permute-done.6
  552.6 0.0 collective-permute-done
  552.6 8.3 %concatenate = bf16[140,3584]{1,0:T(8,128)(2,1)S(1)} concatenate(bf16[12,3584]{1,0:T(8,128)(2,1)S(1)} %collective-permute-done.7, bf16[16,3584]{1,0:T(8,128)(2,1)} %collective-permute-done.6, bf16[16,3584]{1,0:T(8,128)(2,1)S(1)} %collective-permute-done.5, bf16[16,3584]{1,0:T(8,128)(2,1)} %collective-permute-done.4, bf16[16,3584]{1,0:T(8,128)(2,1)} %collective-permute-done.3, ...), dimensions={0} | concatenate | bytes 2121728
  560.9 0.7 dynamic-slice_convert_fusion
  (5 shorter events, 0.1 us)
Async XLA Ops:
  7.2 67.0 %all-gather.7.cloned.1.call-start = ((), (), s32[]{:S(2)}) async-start(), calls=%async_computation.1 | async-start | bytes 3784704 | tf_op jit(solution)/shard_map/all_gather | solution.py:34
  7.9 145.4 %all-gather.5.cloned.1.call-start = ((), (), s32[]{:S(2)}) async-start(), calls=%async_computation | async-start | bytes 8650752 | tf_op jit(solution)/shard_map/all_gather | solution.py:30
  9.4 279.5 %copy-start = (s32[3072]{0:T(1024)}, s32[3072]{0:T(1024)S(1)}, u32[]{:S(2)}) copy-start(s32[3072]{0:T(1024)S(1)} %iota_add_fusion) | copy-start | bytes 36868
  10.1 278.8 %copy-start.3 = (pred[384]{0:T(512)(128)(4,1)}, pred[384]{0:T(512)(128)(4,1)S(1)}, u32[]{:S(2)}) copy-start(pred[384]{0:T(512)(128)(4,1)S(1)} %compare_and_fusion) | copy-start | bytes 1156
  199.7 42.3 %copy-start.7 = (s32[384]{0:T(512)S(1)}, s32[384]{0:T(512)}, u32[]{:S(2)}) copy-start(s32[384]{0:T(512)} %param.10) | copy-start | bytes 4612
  288.2 0.6 copy-start.1
  288.2 0.6 copy-start.2
  288.2 0.6 copy-start.4
  288.8 0.6 copy-start.5
  288.8 0.6 copy-start.6
  472.1 20.0 %collective-permute-start.1 = (bf16[16,3584]{1,0:T(8,128)(2,1)S(1)}, bf16[16,3584]{1,0:T(8,128)(2,1)S(1)}, u32[]{:S(2)}, u32[]{:S(2)}) collective-permute-start(bf16[16,3584]{1,0:T(8,128)(2,1)S(1)} %convert.15), channel_id=1, source_target_pairs={{0,2},{1,3},{2,4},{3,5},{4,6},{5,7},{6,8},{7,9},{8,10},{9,11},{10,... | collective-permute-start | bytes 344072
  473.9 21.7 %collective-permute-start.2 = (bf16[16,3584]{1,0:T(8,128)(2,1)S(1)}, bf16[16,3584]{1,0:T(8,128)(2,1)S(1)}, u32[]{:S(2)}, u32[]{:S(2)}) collective-permute-start(bf16[16,3584]{1,0:T(8,128)(2,1)S(1)} %convert.15), channel_id=1, source_target_pairs={{0,3},{1,4},{2,5},{3,6},{4,7},{5,8},{6,9},{7,10},{8,11},{9,12},{10... | collective-permute-start | bytes 344072
  478.9 11.0 %collective-permute-start.7 = (bf16[12,3584]{1,0:T(8,128)(2,1)S(1)}, bf16[12,3584]{1,0:T(8,128)(2,1)S(1)}, u32[]{:S(2)}, u32[]{:S(2)}) collective-permute-start(bf16[12,3584]{1,0:T(8,128)(2,1)S(1)} %slice.2), channel_id=1, source_target_pairs={{0,8},{1,9},{2,10},{3,11},{4,12},{5,13},{6,14},{7,15},{8,16},{9,17... | collective-permute-start | bytes 258056
  480.2 72.4 %collective-permute-start.3 = (bf16[16,3584]{1,0:T(8,128)(2,1)S(1)}, bf16[16,3584]{1,0:T(8,128)(2,1)}, u32[]{:S(2)}, u32[]{:S(2)}) collective-permute-start(bf16[16,3584]{1,0:T(8,128)(2,1)S(1)} %convert.15), channel_id=1, source_target_pairs={{0,4},{1,5},{2,6},{3,7},{4,8},{5,9},{6,10},{7,11},{8,12},{9,13},{1... | collective-permute-start | bytes 344072
  485.1 67.5 %collective-permute-start.4 = (bf16[16,3584]{1,0:T(8,128)(2,1)S(1)}, bf16[16,3584]{1,0:T(8,128)(2,1)}, u32[]{:S(2)}, u32[]{:S(2)}) collective-permute-start(bf16[16,3584]{1,0:T(8,128)(2,1)S(1)} %convert.15), channel_id=1, source_target_pairs={{0,5},{1,6},{2,7},{3,8},{4,9},{5,10},{6,11},{7,12},{8,13},{9,14},{... | collective-permute-start | bytes 344072
  489.9 62.7 %collective-permute-start.5 = (bf16[16,3584]{1,0:T(8,128)(2,1)S(1)}, bf16[16,3584]{1,0:T(8,128)(2,1)S(1)}, u32[]{:S(2)}, u32[]{:S(2)}) collective-permute-start(bf16[16,3584]{1,0:T(8,128)(2,1)S(1)} %convert.15), channel_id=1, source_target_pairs={{0,6},{1,7},{2,8},{3,9},{4,10},{5,11},{6,12},{7,13},{8,14},{9,15},... | collective-permute-start | bytes 344072
  492.0 60.5 %collective-permute-start.6 = (bf16[16,3584]{1,0:T(8,128)(2,1)S(1)}, bf16[16,3584]{1,0:T(8,128)(2,1)}, u32[]{:S(2)}, u32[]{:S(2)}) collective-permute-start(bf16[16,3584]{1,0:T(8,128)(2,1)S(1)} %convert.15), channel_id=1, source_target_pairs={{0,7},{1,8},{2,9},{3,10},{4,11},{5,12},{6,13},{7,14},{8,15},{9,16}... | collective-permute-start | bytes 344072
  495.6 56.9 %collective-permute-start = (bf16[16,3584]{1,0:T(8,128)(2,1)S(1)}, bf16[16,3584]{1,0:T(8,128)(2,1)}, u32[]{:S(2)}, u32[]{:S(2)}) collective-permute-start(bf16[16,3584]{1,0:T(8,128)(2,1)S(1)} %convert.15), channel_id=1, source_target_pairs={{0,1},{1,2},{2,3},{3,4},{4,5},{5,6},{6,7},{7,8},{8,9},{9,10},{10,1... | collective-permute-start | bytes 344072
Sparse Core Ops, SparseCore 0:
  10.8 63.2 all-gather.6
  77.1 76.1 all-gather.4
where the time goes:
time: 570 us; the launch traced here: 568 us
  blocking collectives  240 us (42%)
  waiting for transfers between devices  126 us (22%)
  matrix products  89.9 us (16%)
  local copies, waits for them, and re-layouts  61.1 us (11%)
  starting transfers between devices  26.1 us (5%)
  between operations  14.2 us (2%)
  other arithmetic  10.9 us (2%)
    unnamed x1, blocking collectives  160 us
    all_gather x1, waiting for transfers between devices, shards(): lax.all_gather(student_hidden, ('grp', 'tp'), axis=0, tiled=True)  64.1 us
    all_gather x1, waiting for transfers between devices, shards(): lax.all_gather(teacher_hidden, ('grp', 'tp'), axis=0, tiled=True)  60.8 us
    unnamed x21, local copies, waits for them, and re-layouts  50 us
    psum x1, blocking collectives, shards(): lax.psum((jnp.sum(teacher_exp, axis=1), jnp.sum(student_exp, axis=1), jnp...  40.2 us
    pmax x1, blocking collectives, shards(): lax.pmax((jnp.max(teacher_logits, axis=1), jnp.max(student_logits, axis=1...  39.4 us
    dot_general x1, matrix products, shards(): jnp.dot(lax.all_gather(teacher_hidden, ('grp', 'tp'), axis=0, tiled=True)...  28.6 us
    unnamed x8, starting transfers between devices  26 us
  transfers between devices with their start and end apart: 10, of which 2 were waited for; matrix products, arithmetic and copies ran while one was open for 13% of the time, Pallas kernels for 0%

commit v1 on v0

v1 whole, which is shorter than its diff:
```python
import functools
import math

import jax
import jax.numpy as jnp
import numpy as np
from jax import lax
from jax.experimental import pallas as pl
from jax.experimental.pallas import tpu as pltpu
from jax.sharding import PartitionSpec as P

MESH = pl.DeviceIdType.MESH
FOLD = 4
SUB = 16
WIDE = 1024
CHUNK_S = 512
SLOTS = 3


def up(value, step):
    return -(-value // step) * step


def windows(rows):
    return [(q * rows // SUB * SUB, up((q + 1) * rows, SUB)) for q in range(FOLD)]


def tables(rows, groups, ring):
    half, line = groups // 2, ring // 2
    owners = [
        (x * 2 + c) * ring + z * 2 + y
        for c in range(2) for x in range(half) for y in range(2) for z in range(line)
    ]
    packed = []
    for q, (low, high) in enumerate(windows(rows)):
        for owner in owners:
            for o in range(low, high):
                r = o - q * rows
                packed.append(owner * rows + r if 0 <= r < rows else -1)
    padded = []
    for owner in owners:
        for o in range(up(rows, SUB)):
            padded.append(owner * rows + o if o < rows else -1)
    return np.array(packed, np.int32)[None, :], np.array(padded, np.int32)[:, None]


def fused(
    rows, groups, ring,
    th, sh, owner_col, label_col, token_row, token_col, t_head, s_head,
    loss_ref, g_out, h_out, gh_ref,
    buf_t, buf_s, heads, acc_t, acc_s, select, piece, hid, grads, place,
    st, stat_col, row_mat, col_mat, rs, rc, rxa, rxb, rya, ryb, rz,
    head_sem, out_sem, send_t, recv_t, send_s, recv_s, send_st, recv_st, send_r, recv_r,
):
    half, line = groups // 2, ring // 2
    devices = groups * ring
    mid = line // 2
    n_t, n_s = buf_t.shape[0], buf_s.shape[0]
    tokens, vocab = acc_t.shape
    grp, tp = lax.axis_index("grp"), lax.axis_index("tp")
    x, c = grp // 2, grp % 2
    z, y = tp // 2, tp % 2
    at_c = (x * 2 + 1 - c, tp)
    at_x = ((1 - x) * 2 + c, tp)
    at_y = (grp, z * 2 + 1 - y)
    at_z = [(grp, lax.rem(z + o, line) * 2 + y) for o in range(1, line)]

    def remote(src, dst, send, recv, device):
        return pltpu.make_async_remote_copy(
            src_ref=src, dst_ref=dst, send_sem=send, recv_sem=recv,
            device_id=device, device_id_type=MESH,
        )

    def load_head(h, slot):
        wide = heads.shape[1]
        narrow = hid.shape[2]

        def t_copy():
            return pltpu.make_async_copy(
                t_head.at[pl.ds(pl.multiple_of(h * wide, wide), wide)], heads.at[slot], head_sem.at[slot])

        def s_copy():
            k = lax.rem(h - n_t, n_s)
            return pltpu.make_async_copy(
                s_head.at[pl.ds(pl.multiple_of(k * narrow, narrow), narrow)],
                heads.at[slot, pl.ds(0, narrow)], head_sem.at[slot])

        return t_copy, s_copy

    def start_head(h):
        slot = lax.rem(h, SLOTS)
        t_copy, s_copy = load_head(h, slot)

        @pl.when(h < n_t)
        def _():
            t_copy().start()

        @pl.when(jnp.logical_and(h >= n_t, h < n_t + 2 * n_s))
        def _():
            s_copy().start()

    start_head(jnp.int32(0))
    start_head(jnp.int32(1))

    barrier = pltpu.get_barrier_semaphore()
    for device in (at_c, at_x, at_y, *at_z):
        pl.semaphore_signal(barrier, inc=1, device_id=device, device_id_type=MESH)
    pl.semaphore_wait(barrier, line + 2)

    def stage(buf, i, send, recv, number):
        b = buf.at[i]
        if number == 0:
            return [
                remote(b.at[c, x, y, z], b.at[c, x, y, z], send.at[i, o], recv.at[i, o], at_z[o])
                for o in range(line - 1)
            ]
        k = line - 1
        first, last = pl.ds(0, mid), pl.ds(mid, line - mid)
        if number == 1:
            one, two = b.at[c, x, y, first], b.at[c, x, y, last]
            return [
                remote(one, one, send.at[i, k], recv.at[i, k], at_y),
                remote(two, two, send.at[i, k + 1], recv.at[i, k + 1], at_x),
            ]
        if number == 2:
            one, two = b.at[c, x, :, first], b.at[c, :, y, last]
            return [
                remote(one, one, send.at[i, k + 2], recv.at[i, k + 2], at_x),
                remote(two, two, send.at[i, k + 3], recv.at[i, k + 3], at_y),
            ]
        return [remote(b.at[c], b.at[c], send.at[i, k + 4], recv.at[i, k + 4], at_c)]

    def advance(buf, i, send, recv, number):
        if number > 0:
            for copy in stage(buf, i, send, recv, number - 1):
                copy.wait_recv()
        if number < 4:
            for copy in stage(buf, i, send, recv, number):
                copy.start()

    def forward(step):
        for number in (0, 3, 2, 1):
            g = step - number

            @pl.when(jnp.logical_and(g >= 0, g < n_t))
            def _():
                advance(buf_t, g, send_t, recv_t, number)

            @pl.when(jnp.logical_and(g >= n_t, g < n_t + n_s))
            def _():
                advance(buf_s, g - n_t, send_s, recv_s, number)

    for i in range(n_t):
        buf_t[i, c, x, y, z] = th[i]
    for i in range(n_s):
        buf_s[i, c, x, y, z] = sh[i]

    spans = windows(rows)

    def set_select(column):
        at = 0
        for low, high in spans:
            size = devices * (high - low)

            @pl.loop(0, tokens // 32)
            def _(r):
                these = pl.ds(pl.multiple_of(r * 32, 32), 32)
                ids = lax.broadcasted_iota(jnp.int32, (32, 1), 0) + r * 32 if column is None else column[these, :]
                hit = ids == token_row[:, at:at + size]
                select[these, at:at + size] = jnp.where(hit, 1.0, 0.0).astype(jnp.bfloat16)

            at += size

    def unfold(buf, i, q):
        low, high = spans[q]
        at = devices * sum(h - l for l, h in spans[:q])
        size = devices * (high - low)
        block = buf[i, :, :, :, :, low:high, :].reshape(size, buf.shape[-1])
        return jnp.dot(select[:, at:at + size], block, preferred_element_type=jnp.float32).astype(jnp.bfloat16)

    tile = 512 if vocab % 512 == 0 else 256

    forward(jnp.int32(0))
    acc_t[...] = jnp.zeros_like(acc_t)
    set_select(owner_col)
    forward(jnp.int32(1))
    acc_s[...] = jnp.zeros_like(acc_s)
    place[...] = jnp.where(
        token_col[...] == lax.broadcasted_iota(jnp.int32, place.shape, 1), 1.0, 0.0
    ).astype(jnp.bfloat16)
    forward(jnp.int32(2))
    forward(jnp.int32(3))

    @pl.loop(0, n_t)
    def _(i):
        forward(i + 4)
        start_head(i + 2)
        advance(buf_t, i, send_t, recv_t, 4)
        width = buf_t.shape[-1]
        for q in range(FOLD):
            piece[:, q * width:(q + 1) * width] = unfold(buf_t, i, q)
        slot = lax.rem(i, SLOTS)
        load_head(i, slot)[0]().wait()

        @pl.loop(0, vocab // tile)
        def _(n):
            cols = pl.ds(pl.multiple_of(n * tile, tile), tile)
            acc_t[:, cols] += jnp.dot(piece[...], heads[slot, :, cols], preferred_element_type=jnp.float32)

    student = hid.shape[2]
    set_select(None)

    @pl.loop(0, n_s)
    def _(i):
        h = i + n_t
        forward(h + 4)
        start_head(h + 2)
        advance(buf_s, i, send_s, recv_s, 4)
        width = buf_s.shape[-1]
        for q in range(FOLD):
            hid[i, :, q * width:(q + 1) * width] = unfold(buf_s, i, q)
        slot = lax.rem(h, SLOTS)
        load_head(h, slot)[1]().wait()

        @pl.loop(0, vocab // tile)
        def _(n):
            cols = pl.ds(pl.multiple_of(n * tile, tile), tile)
            acc_s[:, cols] += jnp.dot(
                hid[i], heads[slot, pl.ds(0, student), cols], preferred_element_type=jnp.float32)

    hid_copy = pltpu.make_async_copy(hid, h_out, out_sem.at[0])
    hid_copy.start()

    base = (grp * ring + tp) * vocab

    @pl.loop(0, tokens // 8)
    def _(r):
        these = pl.ds(pl.multiple_of(r * 8, 8), 8)
        t, s = acc_t[these, :], acc_s[these, :]
        t_top = jnp.max(t, axis=1, keepdims=True)
        s_top = jnp.max(s, axis=1, keepdims=True)
        t_exp, s_exp = jnp.exp(t - t_top), jnp.exp(s - s_top)
        differ = t - s
        hits = label_col[these, :] == lax.broadcasted_iota(jnp.int32, t.shape, 1) + base
        values = [
            t_top, s_top,
            jnp.sum(t_exp, axis=1, keepdims=True),
            jnp.sum(s_exp, axis=1, keepdims=True),
            jnp.sum(t_exp * t, axis=1, keepdims=True),
            jnp.sum(t_exp * differ, axis=1, keepdims=True),
            jnp.sum(s_exp * differ, axis=1, keepdims=True),
            jnp.sum(jnp.where(hits, s, 0.0), axis=1, keepdims=True),
        ]
        lane = lax.broadcasted_iota(jnp.int32, (8, 128), 1)
        out = jnp.zeros((8, 128), jnp.float32)
        for k, value in enumerate(values):
            out = jnp.where(lane == k, value, out)
        stat_col[these, :] = out

    st[0, c, x, y, z] = jnp.transpose(stat_col[...])[0:8, :]
    for number in range(5):
        advance(st, 0, send_st, recv_st, number)

    cells = [(cc, xx, yy) for cc in range(2) for xx in range(half) for yy in range(2)]

    def highest(k, best):
        for cc, xx, yy in cells:
            best = jnp.maximum(best, st[0, cc, xx, yy, k])
        return best

    top = lax.fori_loop(0, line, highest, jnp.full((8, tokens), -jnp.inf, jnp.float32))
    row = lax.broadcasted_iota(jnp.int32, (8, tokens), 0)
    of_student = jnp.logical_or(row == 3, row == 6)

    def gathered(k, sums):
        for cc, xx, yy in cells:
            one = st[0, cc, xx, yy, k]
            shift = jnp.exp(one - top)
            scale = jnp.where(of_student, shift[1:2, :], jnp.where(row == 7, 1.0, shift[0:1, :]))
            sums = sums + one * scale
        return sums

    sums = lax.fori_loop(0, line, gathered, jnp.zeros((8, tokens), jnp.float32))
    t_total, s_total, t_moment, forward_moment, reverse_moment, label_logit = (
        sums[k:k + 1, :] for k in range(2, 8))
    t_lse = top[0:1] + jnp.log(t_total)
    s_lse = top[1:2] + jnp.log(s_total)
    weight = (t_lse - t_moment / t_total) / math.log(vocab * devices)
    ahead = forward_moment / t_total - t_lse + s_lse
    back = -reverse_moment / s_total - s_lse + t_lse
    loss_ref[...] = weight * ahead + (1.0 - weight) * back + s_lse - label_logit

    row_mat[...] = jnp.zeros_like(row_mat)
    for k, value in enumerate((t_lse, s_lse, weight, back)):
        row_mat[k:k + 1, :] = value
    col_mat[...] = jnp.transpose(row_mat[...])

    @pl.loop(0, tokens // SUB)
    def _(r):
        these = pl.ds(pl.multiple_of(r * SUB, SUB), SUB)
        cols = col_mat[these, :]
        log_t = acc_t[these, :] - cols[:, 0:1]
        log_s = acc_s[these, :] - cols[:, 1:2]
        w, rev = cols[:, 2:3], cols[:, 3:4]
        t_prob, s_prob = jnp.exp(log_t), jnp.exp(log_s)
        hits = label_col[these, :] == lax.broadcasted_iota(jnp.int32, log_t.shape, 1) + base
        mixed = w * (s_prob - t_prob) + (1.0 - w) * s_prob * (log_s - log_t - rev)
        mixed = mixed + s_prob - jnp.where(hits, 1.0, 0.0)
        grads[these, :] = (mixed / tokens).astype(jnp.bfloat16)

    grad_copy = pltpu.make_async_copy(grads, g_out, out_sem.at[1])
    grad_copy.start()

    def back_stage(j, number):
        b = rs.at[j]
        first, last = pl.ds(0, mid), pl.ds(mid, line - mid)
        if number == 0:
            return [remote(b.at[1 - c], rc.at[j], send_r.at[j, 0], recv_r.at[j, 0], at_c)]
        if number == 1:
            return [
                remote(b.at[c, 1 - x, :, first], rxa.at[j], send_r.at[j, 1], recv_r.at[j, 1], at_x),
                remote(b.at[c, :, 1 - y, last], ryb.at[j], send_r.at[j, 2], recv_r.at[j, 2], at_y),
            ]
        if number == 2:
            return [
                remote(b.at[c, x, 1 - y, first], rya.at[j], send_r.at[j, 3], recv_r.at[j, 3], at_y),
                remote(b.at[c, 1 - x, y, last], rxb.at[j], send_r.at[j, 4], recv_r.at[j, 4], at_x),
            ]
        return [
            remote(b.at[c, x, y, lax.rem(z + o + 1, line)], rz.at[j, o],
                   send_r.at[j, 5 + o], recv_r.at[j, 5 + o], at_z[o])
            for o in range(line - 1)
        ]

    def plus(one, two):
        return (one.astype(jnp.float32) + two.astype(jnp.float32)).astype(jnp.bfloat16)

    def back_advance(j, number):
        if number > 0:
            for copy in back_stage(j, number - 1):
                copy.wait_recv()
        if number == 1:
            for k in range(half):
                rs[j, c, k] = plus(rs[j, c, k], rc[j, k])
        elif number == 2:
            rs[j, c, x, :, 0:mid] = plus(rs[j, c, x, :, 0:mid], rxa[j])
            rs[j, c, :, y, mid:] = plus(rs[j, c, :, y, mid:], ryb[j])
        elif number == 3:
            rs[j, c, x, y, 0:mid] = plus(rs[j, c, x, y, 0:mid], rya[j])
            rs[j, c, x, y, mid:] = plus(rs[j, c, x, y, mid:], rxb[j])
        elif number == 4:
            own = rs[j, c, x, y, z].astype(jnp.float32)
            for o in range(line - 1):
                own = own + rz[j, o].astype(jnp.float32)
            gh_ref[j] = own.astype(jnp.bfloat16)
        if number < 4:
            for copy in back_stage(j, number):
                copy.start()

    def back_forward(step):
        for number in (4, 3, 2, 1):
            j = step - number

            @pl.when(jnp.logical_and(j >= 0, j < n_s))
            def _():
                back_advance(j, number)

    pad = up(rows, SUB)

    @pl.loop(0, n_s)
    def _(j):
        h = j + n_t + n_s
        start_head(h + 2)
        slot = lax.rem(h, SLOTS)
        load_head(h, slot)[1]().wait()
        part = lax.dot_general(
            grads[...], heads[slot, pl.ds(0, student), :], (((1,), (1,)), ((), ())),
            preferred_element_type=jnp.float32).astype(jnp.bfloat16)
        size = 2 * line * pad
        for cc in range(2):
            for xx in range(half):
                at = (cc * half + xx) * size
                block = jnp.dot(place[at:at + size, :], part, preferred_element_type=jnp.float32)
                rs[j, cc, xx] = block.astype(jnp.bfloat16).reshape(2, line, pad, student)
        back_advance(j, 0)
        back_forward(j)

    for step in range(4):
        back_forward(jnp.int32(n_s + step))

    @pl.loop(0, n_t)
    def _(i):
        for number in range(4):
            for copy in stage(buf_t, i, send_t, recv_t, number):
                copy.wait_send()

    @pl.loop(0, n_s)
    def _(i):
        for number in range(4):
            for copy in stage(buf_s, i, send_s, recv_s, number):
                copy.wait_send()
            for copy in back_stage(i, number):
                copy.wait_send()

    for number in range(4):
        for copy in stage(st, 0, send_st, recv_st, number):
            copy.wait_send()
    hid_copy.wait()
    grad_copy.wait()


def head_kernel(hid, grads, out):
    out[...] = lax.dot_general(
        hid[0], grads[...], (((0,), (0,)), ((), ())), preferred_element_type=jnp.float32
    ).astype(jnp.bfloat16)


def fold(hidden, chunk, block):
    rows, dim = hidden.shape
    parts = dim // chunk
    folded = hidden.reshape(rows, parts, FOLD, chunk // FOLD).transpose(1, 2, 0, 3)
    folded = folded.reshape(parts, FOLD * rows, chunk // FOLD)
    return jnp.pad(folded, ((0, 0), (0, block - FOLD * rows), (0, 0)))


def shards(groups, ring, teacher_hidden, teacher_head, student_hidden, student_head, labels, owner_map):
    rows, t_dim = teacher_hidden.shape
    s_dim, vocab = student_head.shape
    tokens = labels.shape[0]
    half, line, devices = groups // 2, ring // 2, groups * ring
    mid = line // 2
    block, pad = up(FOLD * rows, SUB), up(rows, SUB)
    chunk_t = WIDE if vocab > WIDE else CHUNK_S
    n_t, n_s = t_dim // chunk_t, s_dim // CHUNK_S
    packed, padded = tables(rows, groups, ring)
    vmem = pl.BlockSpec(memory_space=pltpu.VMEM)
    anywhere = pl.BlockSpec(memory_space=pl.ANY)
    bf, f32 = jnp.bfloat16, jnp.float32
    dma = pltpu.SemaphoreType.DMA
    cube = (2, half, 2, line)
    loss, grads, hid, mine = pl.pallas_call(
        functools.partial(fused, rows, groups, ring),
        out_shape=(
            jax.ShapeDtypeStruct((1, tokens), f32),
            jax.ShapeDtypeStruct((tokens, vocab), bf),
            jax.ShapeDtypeStruct((n_s, tokens, CHUNK_S), bf),
            jax.ShapeDtypeStruct((n_s, pad, CHUNK_S), bf),
        ),
        in_specs=[vmem] * 6 + [anywhere] * 2,
        out_specs=(vmem, anywhere, anywhere, vmem),
        scratch_shapes=[
            pltpu.VMEM((n_t, *cube, block, chunk_t // FOLD), bf),
            pltpu.VMEM((n_s, *cube, block, CHUNK_S // FOLD), bf),
            pltpu.VMEM((SLOTS, chunk_t, vocab), bf),
            pltpu.VMEM((tokens, vocab), f32),
            pltpu.VMEM((tokens, vocab), f32),
            pltpu.VMEM((tokens, packed.shape[1]), bf),
            pltpu.VMEM((tokens, chunk_t), bf),
            pltpu.VMEM((n_s, tokens, CHUNK_S), bf),
            pltpu.VMEM((tokens, vocab), bf),
            pltpu.VMEM((devices * pad, tokens), bf),
            pltpu.VMEM((1, *cube, 8, tokens), f32),
            pltpu.VMEM((tokens, 128), f32),
            pltpu.VMEM((128, tokens), f32),
            pltpu.VMEM((tokens, 128), f32),
            pltpu.VMEM((n_s, *cube, pad, CHUNK_S), bf),
            pltpu.VMEM((n_s, half, 2, line, pad, CHUNK_S), bf),
            pltpu.VMEM((n_s, 2, mid, pad, CHUNK_S), bf),
            pltpu.VMEM((n_s, line - mid, pad, CHUNK_S), bf),
            pltpu.VMEM((n_s, mid, pad, CHUNK_S), bf),
            pltpu.VMEM((n_s, half, line - mid, pad, CHUNK_S), bf),
            pltpu.VMEM((n_s, line - 1, pad, CHUNK_S), bf),
            dma((SLOTS,)), dma((2,)),
            dma((n_t, line + 4)), dma((n_t, line + 4)),
            dma((n_s, line + 4)), dma((n_s, line + 4)),
            dma((1, line + 4)), dma((1, line + 4)),
            dma((n_s, line + 4)), dma((n_s, line + 4)),
        ],
        compiler_params=pltpu.CompilerParams(
            collective_id=0, has_side_effects=True, vmem_limit_bytes=62 * 2**20),
        cost_estimate=pl.CostEstimate(
            flops=2 * tokens * vocab * (t_dim + 2 * s_dim),
            bytes_accessed=2 * vocab * (t_dim + 2 * s_dim), transcendentals=4 * tokens * vocab),
    )(
        fold(teacher_hidden, chunk_t, block), fold(student_hidden, CHUNK_S, block),
        owner_map[:, None], labels[:, None], jnp.asarray(packed), jnp.asarray(padded),
        teacher_head, student_head,
    )
    grad_head = pl.pallas_call(
        head_kernel,
        out_shape=jax.ShapeDtypeStruct((s_dim, vocab), bf),
        grid=(n_s,),
        in_specs=[
            pl.BlockSpec((1, tokens, CHUNK_S), lambda i: (i, 0, 0)),
            pl.BlockSpec((tokens, vocab), lambda i: (0, 0)),
        ],
        out_specs=pl.BlockSpec((CHUNK_S, vocab), lambda i: (i, 0)),
        compiler_params=pltpu.CompilerParams(vmem_limit_bytes=40 * 2**20),
        cost_estimate=pl.CostEstimate(
            flops=2 * tokens * vocab * s_dim, bytes_accessed=2 * vocab * s_dim, transcendentals=0),
    )(hid, grads)
    position = lax.axis_index("grp") * ring + lax.axis_index("tp")
    token_loss = lax.dynamic_slice_in_dim(loss[0], position * rows, rows)
    grad_hidden = mine[:, :rows, :].transpose(1, 0, 2).reshape(rows, s_dim)
    return token_loss, grad_head, grad_hidden


def solution(mesh):
    groups, ring = mesh.shape["grp"], mesh.shape["tp"]
    in_specs = (
        P(("grp", "tp"), None),
        P(None, ("grp", "tp")),
        P(("grp", "tp"), None),
        P(None, ("grp", "tp")),
        P(),
        P(),
    )
    out_specs = (P(("grp", "tp")), P(None, ("grp", "tp")), P(("grp", "tp"), None))
    return jax.shard_map(
        functools.partial(shards, groups, ring),
        mesh=mesh, in_specs=in_specs, out_specs=out_specs, check_vma=False)
```

time: 570 us -> 186 us (0.33)
  blocking collectives: 240 us -> 0 us
  Pallas kernels: 0 us -> 173 us
  waiting for transfers between devices: 126 us -> 0 us
  matrix products: 89.9 us -> 0 us
  local copies, waits for them, and re-layouts: 61.1 us -> 12.8 us
  starting transfers between devices: 26.1 us -> 0 us
  between operations: 14.2 us -> 0.68 us
  other arithmetic: 10.9 us -> 0 us
    pallas_call x0 -> x2, Pallas kernels: none -> 173 us  [the longest x1 158 us: shards(): pl.pallas_call(functools.partial(fused, rows, groups, ring), out_shape=(j...]
    unnamed x1 -> x0, blocking collectives: 160 us -> none
    all_gather x2 -> x0, waiting for transfers between devices: 125 us -> none  [the longest x1 64.1 us: shards(): lax.all_gather(student_hidden, ('grp', 'tp'), axis=0, tiled=True)]
    dot_general x4 -> x0, matrix products: 89.9 us -> none  [the longest x1 28.6 us: shards(): jnp.dot(lax.all_gather(teacher_hidden, ('grp', 'tp'), axis=0, tiled=True)...]
    unnamed x21 -> x6, local copies, waits for them, and re-layouts: 50 us -> 4.15 us
    psum x1 -> x0, blocking collectives: 40.2 us -> none  [shards(): lax.psum((jnp.sum(teacher_exp, axis=1), jnp.sum(student_exp, axis=1), jnp...]
    pmax x1 -> x0, blocking collectives: 39.4 us -> none  [shards(): lax.pmax((jnp.max(teacher_logits, axis=1), jnp.max(student_logits, axis=1...]
    unnamed x8 -> x0, starting transfers between devices: 26 us -> none
  transfers between devices with their start and end apart: 10 -> 0, of which waited for: 2 -> 0; matrix products, arithmetic and copies ran while one was open for 13% -> 0% of each run, Pallas kernels for 0% -> 0%
where the time goes in v1:
time: 186 us
  Pallas kernels  173 us (93%)
  local copies, waits for them, and re-layouts  12.8 us (7%)
    pallas_call x1, Pallas kernels, shards(): pl.pallas_call(functools.partial(fused, rows, groups, ring), out_shape=(j...  158 us
    pallas_call x1, Pallas kernels, shards(): pl.pallas_call(head_kernel, out_shape=jax.ShapeDtypeStruct((s_dim, vocab)...  14.5 us
    unnamed x6, local copies, waits for them, and re-layouts  4.15 us

profile of v1, /device:TPU:0, one launch (start us, length us, event | category | flops | bytes accessed | tf_op | source)
XLA Modules:
  0.0 186.1 jit_solution(2719937231522928237)
XLA Ops:
  0.6 0.9 reshape.24
  1.6 0.7 copy.22.sh
  2.3 1.1 reshape.22
  3.4 0.7 copy.21.th
  4.1 1.5 broadcast_in_dim.9.label_col
  5.6 1.5 broadcast_in_dim.8.owner_col
  7.1 158.1 %shard_map.103 = (f32[1,384]{1,0:T(1,128)}, bf16[384,3072]{1,0:T(8,128)(2,1)}, bf16[7,384,512]{2,1,0:T(8,128)(2,1)}, bf16[7,16,512]{2,1,0:T(8,128)(2,1)}) custom-call(bf16[8,48,256]{2,1,0:T(8,128)(2,1)} %copy.21.th, bf16[7,48,128]{2,1,0:T(8,128)(2,1)} %copy.22.sh, s32[384,1]{1,0:T(8,128)} %broadcast_in_dim.8.owner_col, s32[384,1]{1,0:T(8,128)} %broadcast_in_dim.9.label_col, ...), custom_call_target="tpu_custom_call" | custom-call | flops 36238786560 | bytes 94371840 | tf_op jit(solution)/shard_map/pallas_call | solution.py:441
  165.1 1.3 dynamic-slice_bitcast_fusion
  166.4 0.9 slice_bitcast_fusion
  167.3 0.1 copy.25
  167.4 0.7 copy.26
  168.1 0.0 copy-start
  168.1 1.8 copy-done
  169.9 0.0 copy-start.1
  169.9 1.7 copy-done.1
  171.5 14.5 %shard_map.104 = bf16[3584,3072]{1,0:T(8,128)(2,1)} custom-call(bf16[7,384,512]{2,1,0:T(8,128)(2,1)S(1)} %copy-done, bf16[384,3072]{1,0:T(8,128)(2,1)S(1)} %copy-done.1), custom_call_target="tpu_custom_call" | custom-call | flops 8455716864 | bytes 22020096 | tf_op jit(solution)/shard_map/pallas_call | solution.py:489
  (3 shorter events, 0.1 us)
Async XLA Ops:
  168.1 1.8 copy-start
  169.9 1.7 copy-start.1

commit v2 on v1

--- a/solution.py
+++ b/solution.py
@@ -178,7 +178,7 @@
         block = buf[i, :, :, :, :, low:high, :].reshape(size, buf.shape[-1])
         return jnp.dot(select[:, at:at + size], block, preferred_element_type=jnp.float32).astype(jnp.bfloat16)
 
-    tile = 512 if vocab % 512 == 0 else 256
+    tile = 1024 if vocab % 1024 == 0 else 256
 
     forward(jnp.int32(0))
     acc_t[...] = jnp.zeros_like(acc_t)
@@ -233,7 +233,7 @@
 
     base = (grp * ring + tp) * vocab
 
-    @pl.loop(0, tokens // 8)
+    @pl.loop(0, tokens // 8, unroll=4)
     def _(r):
         these = pl.ds(pl.multiple_of(r * 8, 8), 8)
         t, s = acc_t[these, :], acc_s[these, :]
@@ -295,7 +295,7 @@
         row_mat[k:k + 1, :] = value
     col_mat[...] = jnp.transpose(row_mat[...])
 
-    @pl.loop(0, tokens // SUB)
+    @pl.loop(0, tokens // SUB, unroll=2)
     def _(r):
         these = pl.ds(pl.multiple_of(r * SUB, SUB), SUB)
         cols = col_mat[these, :]
@@ -306,7 +306,7 @@
         hits = label_col[these, :] == lax.broadcasted_iota(jnp.int32, log_t.shape, 1) + base
         mixed = w * (s_prob - t_prob) + (1.0 - w) * s_prob * (log_s - log_t - rev)
         mixed = mixed + s_prob - jnp.where(hits, 1.0, 0.0)
-        grads[these, :] = (mixed / tokens).astype(jnp.bfloat16)
+        grads[these, :] = (mixed * (1.0 / tokens)).astype(jnp.bfloat16)
 
     grad_copy = pltpu.make_async_copy(grads, g_out, out_sem.at[1])
     grad_copy.start()

time: 186 us -> 176 us (0.946)
  Pallas kernels: 173 us -> 162 us
    pallas_call x1, Pallas kernels: 158 us -> 148 us  [shards(): pl.pallas_call(functools.partial(fused, rows, groups, ring), out_shape=(j...]
where the time goes in v2:
time: 176 us
  Pallas kernels  162 us (92%)
  local copies, waits for them, and re-layouts  12.8 us (7%)
    pallas_call x1, Pallas kernels, shards(): pl.pallas_call(functools.partial(fused, rows, groups, ring), out_shape=(j...  148 us
    pallas_call x1, Pallas kernels, shards(): pl.pallas_call(head_kernel, out_shape=jax.ShapeDtypeStruct((s_dim, vocab)...  14.5 us
    unnamed x6, local copies, waits for them, and re-layouts  4.15 us

profile of v2, /device:TPU:0, one launch (start us, length us, event | category | flops | bytes accessed | tf_op | source)
XLA Modules:
  0.0 175.6 jit_solution(16037961784803239013)
XLA Ops:
  0.6 0.9 reshape.24
  1.6 0.7 copy.22.sh
  2.3 1.1 reshape.22
  3.4 0.7 copy.21.th
  4.1 1.5 broadcast_in_dim.9.label_col
  5.6 1.5 broadcast_in_dim.8.owner_col
  7.1 147.6 %shard_map.103 = (f32[1,384]{1,0:T(1,128)}, bf16[384,3072]{1,0:T(8,128)(2,1)}, bf16[7,384,512]{2,1,0:T(8,128)(2,1)}, bf16[7,16,512]{2,1,0:T(8,128)(2,1)}) custom-call(bf16[8,48,256]{2,1,0:T(8,128)(2,1)} %copy.21.th, bf16[7,48,128]{2,1,0:T(8,128)(2,1)} %copy.22.sh, s32[384,1]{1,0:T(8,128)} %broadcast_in_dim.8.owner_col, s32[384,1]{1,0:T(8,128)} %broadcast_in_dim.9.label_col, ...), custom_call_target="tpu_custom_call" | custom-call | flops 36238786560 | bytes 94371840 | tf_op jit(solution)/shard_map/pallas_call | solution.py:441
  154.6 1.3 dynamic-slice_bitcast_fusion
  155.9 0.9 slice_bitcast_fusion
  156.8 0.1 copy.25
  156.9 0.7 copy.26
  157.6 0.0 copy-start
  157.6 1.8 %copy-done = bf16[7,384,512]{2,1,0:T(8,128)(2,1)S(1)} copy-done((bf16[7,384,512]{2,1,0:T(8,128)(2,1)S(1)}, bf16[7,384,512]{2,1,0:T(8,128)(2,1)}, u32[]{:S(2)}) %copy-start) | copy-done | bytes 2752536
  159.4 0.0 copy-start.1
  159.4 1.7 copy-done.1
  161.0 14.5 %shard_map.104 = bf16[3584,3072]{1,0:T(8,128)(2,1)} custom-call(bf16[7,384,512]{2,1,0:T(8,128)(2,1)S(1)} %copy-done, bf16[384,3072]{1,0:T(8,128)(2,1)S(1)} %copy-done.1), custom_call_target="tpu_custom_call" | custom-call | flops 8455716864 | bytes 22020096 | tf_op jit(solution)/shard_map/pallas_call | solution.py:489
  (3 shorter events, 0.1 us)
Async XLA Ops:
  157.6 1.8 %copy-start = (bf16[7,384,512]{2,1,0:T(8,128)(2,1)S(1)}, bf16[7,384,512]{2,1,0:T(8,128)(2,1)}, u32[]{:S(2)}) copy-start(bf16[7,384,512]{2,1,0:T(8,128)(2,1)} %get-tuple-element.8.hid) | copy-start | bytes 8257540
  159.4 1.7 copy-start.1
